TPU v7x, 32 devices: a whole 2x2x4 slice. The times are simulated.
32 devices in a mesh: rows: 8 (over z, x), cent: 4 (over y, core).
Axes of the slice: x: 2, y: 2, z: 4, core: 2. Of those that a mesh axis runs over, the one named last changes fastest.
Arguments:
- emb_values: bfloat16 [4096, 1024], P(('cent', 'rows')), may hold values from -6 to 6
- emb_scales: bfloat16 [4096, 8], P(('cent', 'rows')), may hold values from 0.125 to 8, as said below
- coarse_ids: int32 [4, 1024], P(None, 'rows'), may hold values from 0 to 8191, as said below
- centroids: bfloat16 [8192, 1024], P('cent'), may hold values from -6 to 6
- codes_one: int32 [16, 4096], P('rows', 'cent'), may hold values from 0 to 255
- codes_two: int32 [16, 4096], P('rows', 'cent'), may hold values from 0 to 255
- codebook_init: float32 [16, 256, 64], P('rows'), may hold values from -6 to 6
Outputs:
- coarse_gap: float32 [4096], P(('cent', 'rows'))
- codebook_one: float32 [16, 256, 64], P('rows')
- codebook_two: float32 [16, 256, 64], P('rows')
- distortion: float32 [16, 4096], P('rows', 'cent')
Inputs may be any that keep to these rules, and one draw needn't show every extreme that they name: `coarse_ids`: in each aligned block of 128 rows of the flattened ids (the rows of one device), at most 64 ids fall in any one aligned range of 2048 centroids, and exactly 64 fall in some range. `emb_scales`: every scale is a power of two.
All inputs are finite; a program needn't handle non-finite values.
Results may differ from a plain program's by a relative error of at most 0.0003.
Values may be sent and summed in bfloat16 or wider, within the bound.
A program may use at most 64 MiB of HBM per device.

v0:
```python
import jax
import jax.numpy as jnp
from jax import lax
from jax.sharding import PartitionSpec as P

prior_weight = 8.0


def dequantize(values, scales, block_width):
    widened = jnp.repeat(scales.astype(jnp.float32), block_width, axis=1)
    return values.astype(jnp.float32) * widened


def update(totals, counts, prior_book):
    return (totals + prior_weight * prior_book) / (counts + prior_weight)[..., None]


def on_device(emb_values, emb_scales, coarse_ids, centroids, codes_one, codes_two, codebook_init):
    own_rows, feature_width = emb_values.shape
    block_width = feature_width // emb_scales.shape[1]
    cent_index = lax.axis_index("cent")
    local_count = centroids.shape[0]
    sub_width = codebook_init.shape[2]
    codeword_count = codebook_init.shape[1]
    total_subspaces = feature_width // sub_width
    group_values, group_scales = (
        lax.all_gather(emb_values, "cent", axis=0, tiled=True),
        lax.all_gather(emb_scales, "cent", axis=0, tiled=True),
    )
    group_total = group_values.shape[0]
    quantized = dequantize(group_values, group_scales, block_width).astype(jnp.bfloat16)
    cent_squares = jnp.sum(jnp.square(centroids.astype(jnp.float32)), axis=1)
    block_rows = min(512, group_total)

    def nearest_block(row_batch):
        row_squares = jnp.sum(jnp.square(row_batch.astype(jnp.float32)), axis=1)
        cross_terms = lax.dot_general(
            row_batch, centroids, (((1,), (1,)), ((), ())), preferred_element_type=jnp.float32
        )
        distances = row_squares[:, None] - 2.0 * cross_terms + cent_squares[None, :]
        return jnp.min(distances, axis=1)

    local_best = lax.map(
        nearest_block, quantized.reshape(group_total // block_rows, block_rows, feature_width)
    ).reshape(group_total)
    group_best = lax.pmin(local_best, "cent")
    coarse_gap = (
        lax.dynamic_slice_in_dim(group_best, cent_index * own_rows, own_rows) / feature_width
    )
    flat_ids = coarse_ids.reshape(group_total)
    offset = cent_index * local_count
    chosen = flat_ids - offset
    in_block = (chosen >= 0) & (chosen < local_count)
    picked = jnp.take(centroids, jnp.clip(chosen, 0, local_count - 1), axis=0)
    fetched = lax.psum_scatter(
        jnp.where(in_block[:, None], picked, jnp.zeros_like(picked))
        .astype(jnp.float32)
        .astype(jnp.bfloat16),
        "cent",
        scatter_dimension=0,
        tiled=True,
    ).astype(jnp.float32)
    residual = dequantize(emb_values, emb_scales, block_width) - fetched
    stacked = residual.T.reshape(total_subspaces, sub_width, own_rows)
    owned_sub = lax.all_to_all(stacked, "rows", split_axis=0, concat_axis=2, tiled=True)
    codeword_ids = jnp.arange(codeword_count, dtype=jnp.int32)

    def statistics(code_rows):
        onehot = (code_rows[:, None, :] == codeword_ids[None, :, None]).astype(jnp.float32)
        totals = jnp.einsum("skn,sdn->skd", onehot, owned_sub, precision=lax.Precision.HIGHEST)
        counts = jnp.sum(onehot, axis=2)
        return (totals, counts)

    first_totals, first_counts = statistics(codes_one)
    first_stats = lax.psum((first_totals, first_counts), "cent")
    book_one = update(first_stats[0], first_stats[1], codebook_init)
    second_totals, second_counts = statistics(codes_two)
    second_stats = lax.psum((second_totals, second_counts), "cent")
    book_two = update(second_stats[0], second_stats[1], book_one)
    onehot_two = (codes_two[:, None, :] == codeword_ids[None, :, None]).astype(jnp.float32)
    rebuilt = jnp.einsum("skd,skn->sdn", book_two, onehot_two, precision=lax.Precision.HIGHEST)
    difference = owned_sub - rebuilt
    distortion = jnp.sum(difference * difference, axis=1) / sub_width
    return (coarse_gap, book_one, book_two, distortion)


def solution(mesh):
    placed = (
        P(("cent", "rows"), None),
        P(("cent", "rows"), None),
        P(None, "rows"),
        P("cent", None),
        P("rows", "cent"),
        P("rows", "cent"),
        P("rows", None, None),
    )
    return jax.shard_map(
        on_device,
        mesh=mesh,
        in_specs=placed,
        out_specs=(
            P(("cent", "rows")),
            P("rows", None, None),
            P("rows", None, None),
            P("rows", "cent"),
        ),
        check_vma=False,
    )
```

profile of v0, /device:TPU:0, one launch (start us, length us, event | category | flops | bytes accessed | tf_op | source)
XLA Modules:
  0.0 118.1 jit_solution(5850515131709762118)
XLA Ops:
  7.2 0.7 compare_and_fusion
  7.9 0.7 and_bitcast_fusion
  8.6 5.5 %gather_fusion = bf16[512,1024]{1,0:T(8,128)(2,1)S(1)} fusion(bf16[2048,1024]{1,0:T(8,128)(2,1)} %param.10, s32[1024]{0:T(1024)S(1)} %pad_clamp_fusion), kind=kCustom, calls=%fused_computation | custom fusion | bytes 2099200 | tf_op jit(solution)/shard_map/jit(_take)/gather | solution.py:54
  14.1 1.3 %select_select_fusion = bf16[512,1024]{1,0:T(8,128)(2,1)} fusion(bf16[512,1024]{1,0:T(8,128)(2,1)S(1)} %gather_fusion, pred[512]{0:T(512)(128)(4,1)S(1)} %get-tuple-element.25, pred[512]{0:T(512)(128)(4,1)S(1)} %and_bitcast_fusion), kind=kLoop, calls=%fused_computation.18 | loop fusion | flops 1048576 | bytes 2098176 | tf_op jit(solution)/shard_map/jit(_where)/select_n | solution.py:56
  15.4 0.7 all-gather.2.cloned.1.call-update
  16.6 26.6 %reduce-scatter.2.cloned.1.call-done = bf16[128,1024]{1,0:T(8,128)(2,1)} async-done(((bf16[512,1024]{1,0:T(8,128)(2,1)}), bf16[128,1024]{1,0:T(8,128)(2,1)}) %reduce-scatter.2.cloned.1.call-update) | async-done | bytes 262160 | tf_op jit(solution)/shard_map/reduce_scatter | solution.py:55
  43.3 1.1 fusion.11
  44.5 1.0 copy.15
  45.5 5.5 %all-to-all-start = ((f32[16,64,128]{2,1,0:T(8,128)}), f32[16,64,128]{2,1,0:T(8,128)}, u32[]{:S(2)}, u32[]{:S(2)}) async-start(f32[16,64,128]{2,1,0:T(8,128)} %bitcast.5), calls=%async_computation.1 | async-start | bytes 1048576 | tf_op jit(solution)/shard_map/all_to_all | solution.py:65
  51.3 5.2 %all_gather.7 = bf16[512,8]{0,1:T(8,128)(2,1)S(1)} all-gather(bf16[128,8]{0,1:T(8,128)(2,1)S(1)} %copy-done.4), channel_id=1, replica_groups=mesh['rows'=8,'cent'=4] {'cent'}, dimensions={0}, use_global_device_ids=true | all-gather | bytes 10240 | tf_op jit(solution)/shard_map/all_gather | solution.py:28
  56.7 6.5 %all-reduce = (f32[2,256]{1,0:T(2,128)S(1)}, f32[2,256]{1,0:T(2,128)S(1)}) all-reduce(f32[2,256]{1,0:T(2,128)S(1)} %convert_reduce_fusion.1, f32[2,256]{1,0:T(2,128)S(1)} %convert_reduce_fusion), channel_id=1, replica_groups=mesh['rows'=8,'cent'=4] {'cent'}, use_global_device_ids=true, to_apply=%region_7.8 | all-reduce | flops 1024 | bytes 8192 | tf_op jit(solution)/shard_map/psum | solution.py:75
  63.2 3.1 %multiply_reduce_fusion = f32[2048]{0:T(1024)S(1)} fusion(bf16[2048,1024]{1,0:T(8,128)(2,1)} %param.10), kind=kLoop, calls=%fused_computation.1 | loop fusion | flops 6289408 | bytes 4202496 | tf_op jit(solution)/shard_map/reduce_sum | solution.py:32
  66.3 0.6 broadcast_in_dim.44
  66.9 0.6 copy-done.1
  67.5 0.4 multiply_reduce_fusion.1
  67.9 2.9 %fusion.3 = f32[2,256,64]{1,2,0:T(8,128)} fusion(s32[2,1024]{1,0:T(2,128)S(1)} %copy-done.5, f32[8,2,8,8,128]{4,3,2,1,0:T(8,128)} %bitcast.9), kind=kOutput, calls=%fused_computation.11 | convolution fusion | flops 403177472 | bytes 663552 | tf_op jit(solution)/shard_map/skn,sdn->skd/dot_general | solution.py:70
  70.8 2.9 %fusion.2 = f32[2,256,64]{1,2,0:T(8,128)} fusion(s32[2,1024]{1,0:T(2,128)S(1)} %copy-done.6, f32[8,2,8,8,128]{4,3,2,1,0:T(8,128)} %bitcast.9), kind=kOutput, calls=%fused_computation.8 | convolution fusion | flops 403177472 | bytes 663552 | tf_op jit(solution)/shard_map/skn,sdn->skd/dot_general | solution.py:70
  73.7 4.7 %add_reduce_fusion = f32[512]{0:T(512)S(1)} fusion(bf16[2048,1024]{1,0:T(8,128)(2,1)} %param.10, f32[2048]{0:T(1024)S(1)} %multiply_reduce_fusion, f32[512]{0:T(512)S(1)} %multiply_reduce_fusion.1, f32[64,8,8,128]{3,2,1,0:T(8,128)S(1)} %bitcast.39, bf16[512,1024]{1,0:T(8,128)(2,1)S(1)} %copy-done.1), kind=kOutput, calls=%fused_computation.2 | convolution fusion | flops 2153250304 | bytes 7352320 | tf_op jit(solution)/shard_map/while/body/eval_jaxpr/dot_general | solution.py:37
  78.4 6.1 %pmin.7 = f32[512]{0:T(512)S(1)} all-reduce(f32[512]{0:T(512)S(1)} %add_reduce_fusion), channel_id=1, replica_groups=mesh['rows'=8,'cent'=4] {'cent'}, use_global_device_ids=true, to_apply=%region_3.0 | all-reduce | flops 512 | bytes 4096 | tf_op jit(solution)/shard_map/pmin | solution.py:46
  84.5 0.6 dynamic-slice_multiply_fusion
  85.1 22.2 %all-reduce.4.cloned.1.call-done = (f32[2,256,64]{1,2,0:T(8,128)}, f32[2,256,64]{1,2,0:T(8,128)}) async-done(((f32[2,256,64]{1,2,0:T(8,128)}, f32[2,256,64]{1,2,0:T(8,128)}), (f32[2,256,64]{1,2,0:T(8,128)}, f32[2,256,64]{1,2,0:T(8,128)})) %all-reduce.4.cloned.1.call-update) | async-done | bytes 262160 | tf_op jit(solution)/shard_map/psum | solution.py:75
  107.3 1.7 %add_divide_fusion = (f32[2,256,64]{1,2,0:T(8,128)S(1)}, f32[2,256,64]{1,2,0:T(8,128)}) fusion(f32[2,256,64]{1,2,0:T(8,128)} %get-tuple-element.22, f32[2,256]{1,0:T(2,128)S(1)} %get-tuple-element.27, f32[2,256]{1,0:T(2,128)S(1)} %get-tuple-element.28, f32[2,256,64]{1,2,0:T(8,128)} %get-tuple-element.21, f32[2,256,64]{1,2,0:T(8,128)S(1)} %copy-done.2), kind=kLoop, calls=%fused_computation.27 | loop fusion | flops 196608 | bytes 659456 | tf_op jit(solution)/shard_map/div | solution.py:15
  109.0 2.0 %fusion.6 = f32[2,1024]{1,0:T(2,128)S(1)} fusion(f32[2,256,64]{1,2,0:T(8,128)S(1)} %get-tuple-element.23, s32[2,1024]{1,0:T(2,128)S(1)} %copy-done.6, f32[8,2,8,8,128]{4,3,2,1,0:T(8,128)} %bitcast.9), kind=kOutput, calls=%fused_computation.15 | convolution fusion | flops 403568640 | bytes 671744 | tf_op jit(solution)/shard_map/skd,skn->sdn/dot_general | solution.py:81
  111.0 0.6 broadcast_multiply_fusion
  (28 shorter events, 1.2 us)
Async XLA Ops:
  7.2 36.0 %reduce-scatter.2.cloned.1.call-start = ((), (), s32[]{:S(2)}) async-start(), calls=%async_computation.3 | async-start | bytes 1310720 | tf_op jit(solution)/shard_map/reduce_scatter | solution.py:55
  14.1 2.1 %copy-start.4 = (bf16[128,8]{0,1:T(8,128)(2,1)S(1)}, bf16[128,8]{0,1:T(8,128)(2,1)}, u32[]{:S(2)}) copy-start(bf16[128,8]{0,1:T(8,128)(2,1)} %param.8) | copy-start | bytes 6148
  14.1 2.2 %copy-start.5 = (s32[2,1024]{1,0:T(2,128)S(1)}, s32[2,1024]{1,0:T(2,128)}, u32[]{:S(2)}) copy-start(s32[2,1024]{1,0:T(2,128)} %param.11) | copy-start | bytes 24580
  14.1 29.2 %copy-start = (bf16[128,1024]{1,0:T(8,128)(2,1)S(1)}, bf16[128,1024]{1,0:T(8,128)(2,1)}, u32[]{:S(2)}) copy-start(bf16[128,1024]{1,0:T(8,128)(2,1)} %param.7) | copy-start | bytes 786436
  15.4 50.9 %all-gather.2.cloned.1.call-start = ((), (), s32[]{:S(2)}) async-start(), calls=%async_computation.2 | async-start | bytes 1310720 | tf_op jit(solution)/shard_map/all_gather | solution.py:27
  16.6 34.5 %copy-start.6 = (s32[2,1024]{1,0:T(2,128)S(1)}, s32[2,1024]{1,0:T(2,128)}, u32[]{:S(2)}) copy-start(s32[2,1024]{1,0:T(2,128)} %param.12) | copy-start | bytes 24580
  45.5 22.4 %all-to-all-start = ((f32[16,64,128]{2,1,0:T(8,128)}), f32[16,64,128]{2,1,0:T(8,128)}, u32[]{:S(2)}, u32[]{:S(2)}) async-start(f32[16,64,128]{2,1,0:T(8,128)} %bitcast.5), calls=%async_computation.1 | async-start | bytes 1048576 | tf_op jit(solution)/shard_map/all_to_all | solution.py:65
  51.0 56.3 %all-reduce.4.cloned.1.call-start = ((), (), s32[]{:S(2)}) async-start(), calls=%async_computation.4 | async-start | bytes 524288 | tf_op jit(solution)/shard_map/psum | solution.py:75
  66.3 1.2 %copy-start.1 = (bf16[512,1024]{1,0:T(8,128)(2,1)S(1)}, bf16[512,1024]{1,0:T(8,128)(2,1)}, u32[]{:S(2)}) copy-start(bf16[512,1024]{1,0:T(8,128)(2,1)} %all-gather.2.cloned.1.call-done) | copy-start | bytes 3145732
  73.7 33.6 %copy-start.2 = (f32[2,256,64]{1,2,0:T(8,128)S(1)}, f32[2,256,64]{1,2,0:T(8,128)}, u32[]{:S(2)}) copy-start(f32[2,256,64]{1,2,0:T(8,128)} %param.13) | copy-start | bytes 393220
  109.0 2.6 %copy-start.3 = (f32[2,256,64]{1,2,0:T(8,128)}, f32[2,256,64]{1,2,0:T(8,128)S(1)}, u32[]{:S(2)}) copy-start(f32[2,256,64]{1,2,0:T(8,128)S(1)} %get-tuple-element.23) | copy-start | bytes 393220
Sparse Core Ops, SparseCore 0:
  15.5 27.5 reduce-scatter.1
  44.8 16.7 all-gather.1
  73.8 33.4 all-reduce.3
where the time goes:
time: 119 us; the launch traced here: 118 us
  waiting for transfers between devices  49.6 us (42%)
  blocking collectives  17.7 us (15%)
  between operations  13.9 us (12%)
  matrix products  12.5 us (11%)
  other arithmetic  10.7 us (9%)
  local copies, waits for them, and re-layouts  8.15 us (7%)
  starting transfers between devices  5.63 us (5%)
    reduce_scatter x1, waiting for transfers between devices, on_device(): lax.psum_scatter(jnp.where(in_block[:, None], picked, jnp.zeros_like(pick...  26.6 us
    psum x1, waiting for transfers between devices, on_device(): first_stats = lax.psum((first_totals, first_counts), 'cent')  22.2 us
    psum x1, blocking collectives, on_device(): first_stats = lax.psum((first_totals, first_counts), 'cent')  6.51 us
    pmin x1, blocking collectives, on_device(): group_best = lax.pmin(local_best, 'cent')  6.06 us
    dot_general x2, matrix products, statistics(): jnp.einsum('skn,sdn->skd', onehot, owned_sub, precision=lax.Precision.HIG...  5.77 us
    all_to_all x1, starting transfers between devices, on_device(): lax.all_to_all(stacked, 'rows', split_axis=0, concat_axis=2, tiled=True)  5.52 us
    gather x1, local copies, waits for them, and re-layouts, on_device(): picked = jnp.take(centroids, jnp.clip(chosen, 0, local_count - 1), axis=0)  5.46 us
    all_gather x1, blocking collectives, on_device(): lax.all_gather(emb_scales, 'cent', axis=0, tiled=True)  5.18 us
  transfers between devices with their start and end apart: 4, of which 2 were waited for; matrix products, arithmetic and copies ran while one was open for 11% of the time, Pallas kernels for 0%

commit v1 on v0

v1 whole, which is shorter than its diff:
```python
import functools

import jax
import jax.numpy as jnp
from jax import lax
from jax.experimental import pallas as pl
from jax.experimental.pallas import tpu as pltpu
from jax.sharding import PartitionSpec as P

prior_weight = 8.0
MESH = pl.DeviceIdType.MESH
F32, BF16 = jnp.float32, jnp.bfloat16


def dot(a, b, ca, cb):
    return lax.dot_general(a, b, (((ca,), (cb,)), ((), ())), preferred_element_type=F32)


def split(x):
    hi = x.astype(BF16)
    return hi, (x - hi.astype(F32)).astype(BF16)


def kernel(
    C, R,
    val_ref, scale_ref, ids_ref, cent_hbm, one_ref, two_ref, init_ref,
    gap_ref, book1_ref, book2_ref, dist_ref,
    cent, qg, stage, deqc, ids_pad, ids_all, keys, hot, comp_send, comp_recv,
    csq, minbuf, minrecv, xt, oh, st, st_in, st_half, st_out,
    cent_sem, ids_s, ids_r, col_s, col_r, row_s, row_r, pair_s, pair_r,
    comp_s, comp_r, min_s, min_r, s1_s, s1_r, s2_s, s2_r, s3_s, s3_r,
):
    r, c = lax.axis_index("rows"), lax.axis_index("cent")
    N, D = val_ref.shape
    L = cent.shape[0]
    w = stage.shape[2]
    msub = one_ref.shape[0]
    sub = w // msub
    K = init_ref.shape[1]
    lim = comp_send.shape[2]
    Cp = ids_pad.shape[0]
    half = C // 2
    core = lax.rem(c, 2)
    partner = c + 1 - 2 * core
    chip = c // 2

    def at_cent(p):
        return (r, p)

    def at_rows(p):
        return (p, c)

    def remote(src, dst, s, rr, dev):
        return pltpu.make_async_remote_copy(
            src_ref=src, dst_ref=dst, send_sem=s, recv_sem=rr, device_id=dev, device_id_type=MESH
        )

    load = pltpu.make_async_copy(cent_hbm, cent, cent_sem)
    load.start()
    barrier = pltpu.get_barrier_semaphore()
    for d in range(1, C):
        pl.semaphore_signal(barrier, inc=1, device_id=at_cent(lax.rem(c + d, C)), device_id_type=MESH)
    for d in range(1, R):
        pl.semaphore_signal(barrier, inc=1, device_id=at_rows(lax.rem(r + d, R)), device_id_type=MESH)

    width = D // scale_ref.shape[1]
    scales = scale_ref[...].astype(F32)
    squares = jnp.zeros((N, 128), F32)
    for b in range(D // width):
        part = val_ref[:, b * width:(b + 1) * width].astype(F32) * scales[:, b:b + 1]
        part = part.astype(BF16)
        qg[c, :, b * width:(b + 1) * width] = part
        wide = part.astype(F32)
        for e in range(width // 128):
            squares = squares + jnp.square(wide[:, e * 128:(e + 1) * 128])
    for j in range(R):
        stage[j] = qg[c, :, j * w:(j + 1) * w]
    ids_pad[...] = jnp.full(ids_pad.shape, -1, jnp.int32)
    ids_pad[0:C] = ids_ref[...]
    ids_all[r] = ids_pad[...]
    deqc[r] = stage[r]

    pl.semaphore_wait(barrier, C - 1 + R - 1)

    sends = []

    def go(copy):
        copy.start()
        sends.append(copy)

    for d in range(1, R):
        p = lax.rem(r + d, R)
        go(remote(ids_pad, ids_all.at[r], ids_s.at[d], ids_r.at[d], at_rows(p)))
    for e in range(1, half):
        p = lax.rem(c + 2 * e, C)
        go(remote(qg.at[c], qg.at[c], row_s.at[e], row_r.at[e], at_cent(p)))
    go(remote(qg.at[c], qg.at[c], pair_s.at[0], pair_r.at[0], at_cent(partner)))
    for d in range(1, R):
        p = lax.rem(r + d, R)
        go(remote(stage.at[p], deqc.at[r], col_s.at[d], col_r.at[d], at_rows(p)))

    iota_k = lax.broadcasted_iota(jnp.int32, (K, one_ref.shape[1]), 0)
    for t, ref in enumerate((one_ref, two_ref)):
        for m in range(msub):
            oh[t, m] = jnp.where(ref[m:m + 1, :] == iota_k, 1.0, 0.0).astype(BF16)

    for d in range(1, R):
        p = lax.rem(r + R - d, R)
        remote(ids_pad, ids_all.at[p], ids_s.at[d], ids_r.at[d], at_rows(p)).wait_recv()
    ids = ids_all[...].reshape(R * Cp, N)
    before = jnp.where(
        lax.broadcasted_iota(jnp.int32, (N, N), 0) < lax.broadcasted_iota(jnp.int32, (N, N), 1), 1.0, 0.0
    ).astype(BF16)
    for p in range(C):
        mask = (ids >= p * L) & (ids < (p + 1) * L)
        rank = dot(jnp.where(mask, 1.0, 0.0).astype(BF16), before, 1, 0)
        keys[p] = jnp.where(mask, rank, -1.0)

    load.wait()
    iota_slot = lax.broadcasted_iota(jnp.int32, (lim, N), 0).astype(F32)
    iota_cent = lax.broadcasted_iota(jnp.int32, (lim, L), 1)
    if w % 128 == 0:
        columns = cent[:, pl.ds(pl.multiple_of(r * w, 128), w)]
    else:
        per = 128 // w
        columns = cent[:, pl.ds(pl.multiple_of((r // per) * 128, 128), 128)]

    def fetch(p):
        for j in range(R):
            key = keys[c, pl.ds(j * Cp + p, 1), :]
            idrow = ids_all[j, pl.ds(p, 1), :].astype(F32)
            local = jnp.sum(jnp.where(key == iota_slot, idrow - (c * L).astype(F32), 0.0), axis=1, keepdims=True)
            hot[j * lim:(j + 1) * lim, :] = jnp.where(local.astype(jnp.int32) == iota_cent, 1.0, 0.0).astype(BF16)
        got = dot(hot[...], columns, 1, 0)
        if w % 128:
            own = got[:, 0:w]
            for i in range(1, 128 // w):
                own = jnp.where(lax.rem(r, 128 // w) == i, got[:, i * w:(i + 1) * w], own)
            got = own
        return got.astype(BF16).reshape(R, lim, w)

    order = [d for d in range(2, C - 1)] + ([C - 1] if C > 2 else []) + [1]
    for d in order:
        p = lax.rem(c + d, C)
        comp_send[d] = fetch(p)
        go(remote(comp_send.at[d], comp_recv.at[c], comp_s.at[d], comp_r.at[d], at_cent(p)))
    comp_recv[c] = fetch(c)

    chunk = min(256, L)

    def nearest(j, first):
        rows = qg[pl.ds(2 * j, 2)].reshape(2 * N, D)

        def step(i, best):
            at = pl.ds(pl.multiple_of(i * chunk, chunk), chunk)
            block = cent[at, :]
            if first:
                total = jnp.zeros((chunk, 128), F32)
                for e in range(D // 128):
                    total = total + jnp.square(block[:, e * 128:(e + 1) * 128].astype(F32))
                csq[at, :] = jnp.broadcast_to(jnp.sum(total, axis=1, keepdims=True), (chunk, 128))
            cs = csq[at, :]
            far = jnp.concatenate([cs] * (2 * N // 128), axis=1) - 2.0 * dot(block, rows, 1, 1)
            return jnp.minimum(best, jnp.min(far.reshape(chunk // 8, 8, 2 * N), axis=0))

        best = lax.fori_loop(0, L // chunk, step, jnp.full((8, 2 * N), jnp.inf, F32))
        best = jnp.broadcast_to(jnp.min(best, axis=0, keepdims=True), (8, 2 * N))
        minbuf[2 * j] = best[:, 0:N]
        minbuf[2 * j + 1] = best[:, N:2 * N]

    for e in range(1, half):
        p = lax.rem(c + C - 2 * e, C)
        remote(qg.at[p], qg.at[p], row_s.at[e], row_r.at[e], at_cent(p)).wait_recv()
        go(remote(qg.at[p], qg.at[p], pair_s.at[e], pair_r.at[e], at_cent(partner)))
    remote(qg.at[partner], qg.at[partner], pair_s.at[0], pair_r.at[0], at_cent(partner)).wait_recv()
    nearest(chip, True)

    eye = jnp.where(
        lax.broadcasted_iota(jnp.int32, (N, N), 0) == lax.broadcasted_iota(jnp.int32, (N, N), 1), 1.0, 0.0
    ).astype(BF16)
    for d in range(1, R):
        p = lax.rem(r + R - d, R)
        remote(stage.at[p], deqc.at[p], col_s.at[d], col_r.at[d], at_rows(p)).wait_recv()
    for d in range(1, C):
        p = lax.rem(c + C - d, C)
        remote(comp_send.at[d], comp_recv.at[p], comp_s.at[d], comp_r.at[d], at_cent(p)).wait_recv()
    for j in range(R):
        sel = [
            jnp.where(keys[p, pl.ds(j * Cp + c, 1), :] == iota_slot, 1.0, 0.0).astype(BF16) for p in range(C)
        ]
        got = comp_recv[:, j].reshape(C * lim, w)
        fetched = dot(got, jnp.concatenate(sel, axis=0), 0, 0)
        xt[:, j * N:(j + 1) * N] = dot(deqc[j], eye, 0, 0) - fetched

    wide_rows = xt.shape[1]
    ones = jnp.ones((16, wide_rows), BF16)
    for m in range(msub):
        hi, lo = split(xt[m * sub:(m + 1) * sub, :])
        left = jnp.concatenate([hi, lo, ones], axis=0)
        for t in range(2):
            got = dot(left, oh[t, m], 1, 1)
            total = got[0:sub] + got[sub:2 * sub]
            count = got[2 * sub:2 * sub + 8]
            for h in range(2):
                at = slice(h * (K // 2), (h + 1) * (K // 2))
                st[h, t, m * sub:(m + 1) * sub, :] = total[:, at]
                st[h, t, w + 8 * m:w + 8 * m + 8, :] = count[:, at]

    first = remote(st.at[1 - core], st_in, s1_s, s1_r, at_cent(partner))
    first.start()
    first.wait_recv()
    st_half[chip] = st[core] + st_in[...]
    for e in range(1, half):
        p = lax.rem(c + 2 * e, C)
        go(remote(st_half.at[chip], st_half.at[chip], s2_s.at[e], s2_r.at[e], at_cent(p)))
    for e in range(1, half):
        p = lax.rem(partner + C - 2 * e, C)
        remote(qg.at[p], qg.at[p], pair_s.at[e], pair_r.at[e], at_cent(partner)).wait_recv()
        nearest(lax.rem(chip + half - e, half), False)
    for d in range(1, C):
        p = lax.rem(c + d, C)
        go(remote(minbuf.at[p], minrecv.at[c], min_s.at[d], min_r.at[d], at_cent(p)))
    minrecv[c] = minbuf[c]
    for e in range(1, half):
        p = lax.rem(chip + half - e, half)
        remote(st_half.at[p], st_half.at[p], s2_s.at[e], s2_r.at[e], at_cent(partner)).wait_recv()
    total = st_half[0]
    for e in range(1, half):
        total = total + st_half[e]
    st_out[core] = total
    last = remote(st_out.at[core], st_out.at[core], s3_s, s3_r, at_cent(partner))
    last.start()
    last.wait_send()
    remote(st_out.at[1 - core], st_out.at[1 - core], s3_s, s3_r, at_cent(partner)).wait_recv()

    for m in range(msub):
        at = slice(m * sub, (m + 1) * sub)
        row = slice(w + 8 * m, w + 8 * m + 1)

        def stat(t, rows):
            return jnp.concatenate([st_out[0, t, rows, :], st_out[1, t, rows, :]], axis=1)

        book = init_ref[m].T
        for t, ref in enumerate((book1_ref, book2_ref)):
            book = (stat(t, at) + prior_weight * book) / (stat(t, row) + prior_weight)
            ref[m] = book.T
        hi, lo = split(book)
        made = dot(jnp.concatenate([hi, lo], axis=0), oh[1, m], 1, 0)
        off = xt[at, :] - (made[0:sub] + made[sub:2 * sub])
        dist_ref[m:m + 1, :] = jnp.sum(off * off, axis=0, keepdims=True) * (1.0 / sub)

    for d in range(1, C):
        p = lax.rem(c + C - d, C)
        remote(minbuf.at[p], minrecv.at[p], min_s.at[d], min_r.at[d], at_cent(p)).wait_recv()
    best = minrecv[0]
    for p in range(1, C):
        best = jnp.minimum(best, minrecv[p])
    norm = jnp.broadcast_to(jnp.sum(squares, axis=1, keepdims=True), (N, 128)).T
    gap_ref[...] = (best[0:1] + norm[0:1]) * (1.0 / D)

    first.wait_send()
    for copy in sends:
        copy.wait_send()


def on_device(C, R, emb_values, emb_scales, coarse_ids, centroids, codes_one, codes_two, codebook_init):
    N, D = emb_values.shape
    L = centroids.shape[0]
    msub, K, sub = codebook_init.shape
    w = msub * sub
    lim = 2 * N // C
    Cp = max(8, C)
    rows = codes_one.shape[1]
    tall = w + 8 * msub
    vmem = pl.BlockSpec(memory_space=pltpu.VMEM)
    dma = pltpu.SemaphoreType.DMA
    gap, book_one, book_two, distortion = pl.pallas_call(
        functools.partial(kernel, C, R),
        out_shape=(
            jax.ShapeDtypeStruct((1, N), F32),
            jax.ShapeDtypeStruct((msub, K, sub), F32),
            jax.ShapeDtypeStruct((msub, K, sub), F32),
            jax.ShapeDtypeStruct((msub, rows), F32),
        ),
        in_specs=[vmem, vmem, vmem, pl.BlockSpec(memory_space=pl.ANY), vmem, vmem, vmem],
        out_specs=(vmem,) * 4,
        scratch_shapes=[
            pltpu.VMEM((L, D), BF16),
            pltpu.VMEM((C, N, D), BF16),
            pltpu.VMEM((R, N, w), BF16),
            pltpu.VMEM((R, N, w), BF16),
            pltpu.VMEM((Cp, N), jnp.int32),
            pltpu.VMEM((R, Cp, N), jnp.int32),
            pltpu.VMEM((C, R * Cp, N), F32),
            pltpu.VMEM((R * lim, L), BF16),
            pltpu.VMEM((C, R, lim, w), BF16),
            pltpu.VMEM((C, R, lim, w), BF16),
            pltpu.VMEM((L, 128), F32),
            pltpu.VMEM((C, 8, N), F32),
            pltpu.VMEM((C, 8, N), F32),
            pltpu.VMEM((w, rows), F32),
            pltpu.VMEM((2, msub, K, rows), BF16),
            pltpu.VMEM((2, 2, tall, K // 2), F32),
            pltpu.VMEM((2, tall, K // 2), F32),
            pltpu.VMEM((C // 2, 2, tall, K // 2), F32),
            pltpu.VMEM((2, 2, tall, K // 2), F32),
            dma,
            dma((R,)), dma((R,)), dma((R,)), dma((R,)),
            dma((C // 2,)), dma((C // 2,)), dma((C // 2,)), dma((C // 2,)),
            dma((C,)), dma((C,)), dma((C,)), dma((C,)),
            dma, dma,
            dma((C // 2,)), dma((C // 2,)),
            dma, dma,
        ],
        compiler_params=pltpu.CompilerParams(
            collective_id=0, has_side_effects=True, vmem_limit_bytes=48 * 1024 * 1024
        ),
    )(emb_values, emb_scales, coarse_ids, centroids, codes_one, codes_two, codebook_init)
    return gap.reshape(N), book_one, book_two, distortion


def solution(mesh):
    placed = (
        P(("cent", "rows"), None),
        P(("cent", "rows"), None),
        P(None, "rows"),
        P("cent", None),
        P("rows", "cent"),
        P("rows", "cent"),
        P("rows", None, None),
    )
    return jax.shard_map(
        functools.partial(on_device, mesh.shape["cent"], mesh.shape["rows"]),
        mesh=mesh,
        in_specs=placed,
        out_specs=(
            P(("cent", "rows")),
            P("rows", None, None),
            P("rows", None, None),
            P("rows", "cent"),
        ),
        check_vma=False,
    )
```

time: 119 us -> 39.1 us (0.33)
  waiting for transfers between devices: 49.6 us -> 0 us
  Pallas kernels: 0 us -> 28.4 us
  blocking collectives: 17.7 us -> 0 us
  between operations: 13.9 us -> 0.66 us
  matrix products: 12.5 us -> 0 us
  other arithmetic: 10.7 us -> 0 us
  starting transfers between devices: 5.63 us -> 0 us
  local copies, waits for them, and re-layouts: 8.15 us -> 9.69 us
    pallas_call x0 -> x1, Pallas kernels: none -> 28.4 us  [on_device(): pl.pallas_call(functools.partial(kernel, C, R), out_shape=(jax.ShapeDtype...]
    reduce_scatter x1 -> x0, waiting for transfers between devices: 26.6 us -> none  [on_device(): lax.psum_scatter(jnp.where(in_block[:, None], picked, jnp.zeros_like(pick...]
    psum x1 -> x0, waiting for transfers between devices: 22.2 us -> none  [on_device(): first_stats = lax.psum((first_totals, first_counts), 'cent')]
    dot_general x4 -> x0, matrix products: 12.5 us -> none  [the longest x2 5.77 us: statistics(): jnp.einsum('skn,sdn->skd', onehot, owned_sub, precision=lax.Precision.HIG...]
    unnamed x14 -> x16, local copies, waits for them, and re-layouts: 0.65 us -> 9.69 us
    psum x1 -> x0, blocking collectives: 6.51 us -> none  [on_device(): first_stats = lax.psum((first_totals, first_counts), 'cent')]
    pmin x1 -> x0, blocking collectives: 6.06 us -> none  [on_device(): group_best = lax.pmin(local_best, 'cent')]
    all_to_all x1 -> x0, starting transfers between devices: 5.52 us -> none  [on_device(): lax.all_to_all(stacked, 'rows', split_axis=0, concat_axis=2, tiled=True)]
  transfers between devices with their start and end apart: 4 -> 0, of which waited for: 2 -> 0; matrix products, arithmetic and copies ran while one was open for 11% -> 0% of each run, Pallas kernels for 0% -> 0%
where the time goes in v1:
time: 39.1 us; the launch traced here: 38.8 us
  Pallas kernels  28.4 us (73%)
  local copies, waits for them, and re-layouts  9.69 us (25%)
  between operations  0.66 us (2%)
    pallas_call x1, Pallas kernels, on_device(): pl.pallas_call(functools.partial(kernel, C, R), out_shape=(jax.ShapeDtype...  28.4 us
    unnamed x16, local copies, waits for them, and re-layouts  9.69 us

profile of v1, /device:TPU:0, one launch (start us, length us, event | category | flops | bytes accessed | tf_op | source)
XLA Modules:
  0.0 38.8 jit_solution(4880662491406427533)
XLA Ops:
  0.6 0.8 %copy.11.scale_ref = bf16[128,8]{1,0:T(8,128)(2,1)S(1)} copy(bf16[128,8]{0,1:T(8,128)(2,1)} %param.8) | data formatting | bytes 4096 | tf_op args[1]
  1.4 1.0 %copy.12.init_ref = f32[2,256,64]{2,1,0:T(8,128)S(1)} copy(f32[2,256,64]{1,2,0:T(8,128)} %param.13) | data formatting | bytes 262144 | tf_op args[6]
  2.5 0.0 copy-start
  2.5 2.2 %copy-done = bf16[2048,1024]{1,0:T(8,128)(2,1)S(1)} copy-done((bf16[2048,1024]{1,0:T(8,128)(2,1)S(1)}, bf16[2048,1024]{1,0:T(8,128)(2,1)}, u32[]{:S(2)}) %copy-start) | copy-done | bytes 4194328
  4.7 0.0 copy-start.1
  4.7 0.9 %copy-done.1 = bf16[128,1024]{1,0:T(8,128)(2,1)S(1)} copy-done((bf16[128,1024]{1,0:T(8,128)(2,1)S(1)}, bf16[128,1024]{1,0:T(8,128)(2,1)}, u32[]{:S(2)}) %copy-start.1) | copy-done | bytes 262168
  5.6 0.0 copy-start.2
  5.6 0.7 %copy-done.2 = s32[2,1024]{1,0:T(2,128)S(1)} copy-done((s32[2,1024]{1,0:T(2,128)S(1)}, s32[2,1024]{1,0:T(2,128)}, u32[]{:S(2)}) %copy-start.2) | copy-done | bytes 8216
  6.3 0.0 copy-start.3
  6.3 0.7 %copy-done.3 = s32[2,1024]{1,0:T(2,128)S(1)} copy-done((s32[2,1024]{1,0:T(2,128)S(1)}, s32[2,1024]{1,0:T(2,128)}, u32[]{:S(2)}) %copy-start.3) | copy-done | bytes 8216
  7.0 0.0 copy-start.4
  7.0 0.7 %copy-done.4 = s32[4,128]{1,0:T(4,128)S(1)} copy-done((s32[4,128]{1,0:T(4,128)S(1)}, s32[4,128]{1,0:T(4,128)}, u32[]{:S(2)}) %copy-start.4) | copy-done | bytes 2072
  7.7 28.4 %shard_map.102 = (f32[1,128]{1,0:T(1,128)S(1)}, f32[2,256,64]{2,1,0:T(8,128)S(1)}, f32[2,256,64]{2,1,0:T(8,128)S(1)}, f32[2,1024]{1,0:T(2,128)S(1)}) custom-call(bf16[128,1024]{1,0:T(8,128)(2,1)S(1)} %copy-done.1, bf16[128,8]{1,0:T(8,128)(2,1)S(1)} %copy.11.scale_ref, s32[4,128]{1,0:T(4,128)S(1)} %copy-done.4, bf16[2048,1024]{1,0:T(8,128)(2,1)S(1)} %copy-done, ...), custom_call_target="tpu_custom_call" | custom-call | tf_op jit(solution)/shard_map/pallas_call | solution.py:277
  36.1 0.8 %copy.13 = f32[2,256,64]{1,2,0:T(8,128)} copy(f32[2,256,64]{2,1,0:T(8,128)S(1)} %get-tuple-element.13) | data formatting | bytes 262144
  36.9 0.8 %copy.14 = f32[2,256,64]{1,2,0:T(8,128)} copy(f32[2,256,64]{2,1,0:T(8,128)S(1)} %get-tuple-element.14) | data formatting | bytes 262144
  37.6 0.5 %copy.17 = f32[128]{0:T(128)} copy(f32[128]{0:T(128)S(1)} %bitcast.1) | data formatting | bytes 1024
  38.2 0.6 %copy.18 = f32[2,1024]{1,0:T(2,128)} copy(f32[2,1024]{1,0:T(2,128)S(1)} %get-tuple-element.23) | data formatting | bytes 16384
Async XLA Ops:
  2.5 2.2 %copy-start = (bf16[2048,1024]{1,0:T(8,128)(2,1)S(1)}, bf16[2048,1024]{1,0:T(8,128)(2,1)}, u32[]{:S(2)}) copy-start(bf16[2048,1024]{1,0:T(8,128)(2,1)} %cent_hbm.1) | copy-start | bytes 12582916
  4.7 0.9 %copy-start.1 = (bf16[128,1024]{1,0:T(8,128)(2,1)S(1)}, bf16[128,1024]{1,0:T(8,128)(2,1)}, u32[]{:S(2)}) copy-start(bf16[128,1024]{1,0:T(8,128)(2,1)} %val_ref.1) | copy-start | bytes 786436
  5.6 0.7 %copy-start.2 = (s32[2,1024]{1,0:T(2,128)S(1)}, s32[2,1024]{1,0:T(2,128)}, u32[]{:S(2)}) copy-start(s32[2,1024]{1,0:T(2,128)} %one_ref.1) | copy-start | bytes 24580
  6.3 0.7 %copy-start.3 = (s32[2,1024]{1,0:T(2,128)S(1)}, s32[2,1024]{1,0:T(2,128)}, u32[]{:S(2)}) copy-start(s32[2,1024]{1,0:T(2,128)} %two_ref.1) | copy-start | bytes 24580
  7.0 0.7 %copy-start.4 = (s32[4,128]{1,0:T(4,128)S(1)}, s32[4,128]{1,0:T(4,128)}, u32[]{:S(2)}) copy-start(s32[4,128]{1,0:T(4,128)} %ids_ref.1) | copy-start | bytes 6148

commit v2 on v1

--- a/solution.py
+++ b/solution.py
@@ -23,11 +23,12 @@
 
 def kernel(
     C, R,
-    val_ref, scale_ref, ids_ref, cent_hbm, one_ref, two_ref, init_ref,
+    val_hbm, scale_hbm, ids_hbm, cent_hbm, one_hbm, two_hbm, init_hbm,
     gap_ref, book1_ref, book2_ref, dist_ref,
+    val_ref, scale_ref, ids_ref, one_ref, two_ref, init_ref,
     cent, qg, stage, deqc, ids_pad, ids_all, keys, hot, comp_send, comp_recv,
     csq, minbuf, minrecv, xt, oh, st, st_in, st_half, st_out,
-    cent_sem, ids_s, ids_r, col_s, col_r, row_s, row_r, pair_s, pair_r,
+    in_sem, cent_sem, ids_s, ids_r, col_s, col_r, row_s, row_r, pair_s, pair_r,
     comp_s, comp_r, min_s, min_r, s1_s, s1_r, s2_s, s2_r, s3_s, s3_r,
 ):
     r, c = lax.axis_index("rows"), lax.axis_index("cent")
@@ -36,7 +37,7 @@
     w = stage.shape[2]
     msub = one_ref.shape[0]
     sub = w // msub
-    K = init_ref.shape[1]
+    K = init_ref.shape[2]
     lim = comp_send.shape[2]
     Cp = ids_pad.shape[0]
     half = C // 2
@@ -55,6 +56,15 @@
             src_ref=src, dst_ref=dst, send_sem=s, recv_sem=rr, device_id=dev, device_id_type=MESH
         )
 
+    loads = [
+        pltpu.make_async_copy(src, dst, in_sem.at[i])
+        for i, (src, dst) in enumerate((
+            (val_hbm, val_ref), (scale_hbm, scale_ref), (ids_hbm, ids_ref),
+            (one_hbm, one_ref), (two_hbm, two_ref), (init_hbm, init_ref),
+        ))
+    ]
+    for copy in loads:
+        copy.start()
     load = pltpu.make_async_copy(cent_hbm, cent, cent_sem)
     load.start()
     barrier = pltpu.get_barrier_semaphore()
@@ -63,11 +73,18 @@
     for d in range(1, R):
         pl.semaphore_signal(barrier, inc=1, device_id=at_rows(lax.rem(r + d, R)), device_id_type=MESH)
 
-    width = D // scale_ref.shape[1]
-    scales = scale_ref[...].astype(F32)
+    blocks = scale_ref.shape[0]
+    width = D // blocks
+    spread = jnp.where(
+        lax.broadcasted_iota(jnp.int32, (blocks, D), 1) // width
+        == lax.broadcasted_iota(jnp.int32, (blocks, D), 0), 1.0, 0.0
+    ).astype(BF16)
+    for copy in loads[:3]:
+        copy.wait()
+    scales = dot(scale_ref[...], spread, 0, 0)
     squares = jnp.zeros((N, 128), F32)
     for b in range(D // width):
-        part = val_ref[:, b * width:(b + 1) * width].astype(F32) * scales[:, b:b + 1]
+        part = val_ref[:, b * width:(b + 1) * width].astype(F32) * scales[:, b * width:(b + 1) * width]
         part = part.astype(BF16)
         qg[c, :, b * width:(b + 1) * width] = part
         wide = part.astype(F32)
@@ -98,11 +115,6 @@
     for d in range(1, R):
         p = lax.rem(r + d, R)
         go(remote(stage.at[p], deqc.at[r], col_s.at[d], col_r.at[d], at_rows(p)))
-
-    iota_k = lax.broadcasted_iota(jnp.int32, (K, one_ref.shape[1]), 0)
-    for t, ref in enumerate((one_ref, two_ref)):
-        for m in range(msub):
-            oh[t, m] = jnp.where(ref[m:m + 1, :] == iota_k, 1.0, 0.0).astype(BF16)
 
     for d in range(1, R):
         p = lax.rem(r + R - d, R)
@@ -146,6 +158,13 @@
         go(remote(comp_send.at[d], comp_recv.at[c], comp_s.at[d], comp_r.at[d], at_cent(p)))
     comp_recv[c] = fetch(c)
 
+    for copy in loads[3:]:
+        copy.wait()
+    iota_k = lax.broadcasted_iota(jnp.int32, (K, one_ref.shape[1]), 0)
+    for t, ref in enumerate((one_ref, two_ref)):
+        for m in range(msub):
+            oh[t, m] = jnp.where(ref[m:m + 1, :] == iota_k, 1.0, 0.0).astype(BF16)
+
     chunk = min(256, L)
 
     def nearest(j, first):
@@ -240,10 +259,10 @@
         def stat(t, rows):
             return jnp.concatenate([st_out[0, t, rows, :], st_out[1, t, rows, :]], axis=1)
 
-        book = init_ref[m].T
+        book = init_ref[m]
         for t, ref in enumerate((book1_ref, book2_ref)):
             book = (stat(t, at) + prior_weight * book) / (stat(t, row) + prior_weight)
-            ref[m] = book.T
+            ref[m] = book
         hi, lo = split(book)
         made = dot(jnp.concatenate([hi, lo], axis=0), oh[1, m], 1, 0)
         off = xt[at, :] - (made[0:sub] + made[sub:2 * sub])
@@ -263,28 +282,46 @@
         copy.wait_send()
 
 
+def write_out(a0, a1, a2, a3, b0, b1, b2, b3, sems):
+    copies = [
+        pltpu.make_async_copy(a, b, sems.at[i]) for i, (a, b) in enumerate(((a0, b0), (a1, b1), (a2, b2), (a3, b3)))
+    ]
+    for copy in copies:
+        copy.start()
+    for copy in copies:
+        copy.wait()
+
+
 def on_device(C, R, emb_values, emb_scales, coarse_ids, centroids, codes_one, codes_two, codebook_init):
     N, D = emb_values.shape
     L = centroids.shape[0]
     msub, K, sub = codebook_init.shape
+    blocks = emb_scales.shape[1]
     w = msub * sub
     lim = 2 * N // C
     Cp = max(8, C)
     rows = codes_one.shape[1]
     tall = w + 8 * msub
     vmem = pl.BlockSpec(memory_space=pltpu.VMEM)
+    hbm = pl.BlockSpec(memory_space=pltpu.HBM)
     dma = pltpu.SemaphoreType.DMA
-    gap, book_one, book_two, distortion = pl.pallas_call(
+    results = pl.pallas_call(
         functools.partial(kernel, C, R),
         out_shape=(
             jax.ShapeDtypeStruct((1, N), F32),
-            jax.ShapeDtypeStruct((msub, K, sub), F32),
-            jax.ShapeDtypeStruct((msub, K, sub), F32),
+            jax.ShapeDtypeStruct((msub, sub, K), F32),
+            jax.ShapeDtypeStruct((msub, sub, K), F32),
             jax.ShapeDtypeStruct((msub, rows), F32),
         ),
-        in_specs=[vmem, vmem, vmem, pl.BlockSpec(memory_space=pl.ANY), vmem, vmem, vmem],
+        in_specs=[hbm] * 7,
         out_specs=(vmem,) * 4,
         scratch_shapes=[
+            pltpu.VMEM((N, D), BF16),
+            pltpu.VMEM((blocks, N), BF16),
+            pltpu.VMEM((C, N), jnp.int32),
+            pltpu.VMEM((msub, rows), jnp.int32),
+            pltpu.VMEM((msub, rows), jnp.int32),
+            pltpu.VMEM((msub, sub, K), F32),
             pltpu.VMEM((L, D), BF16),
             pltpu.VMEM((C, N, D), BF16),
             pltpu.VMEM((R, N, w), BF16),
@@ -304,7 +341,7 @@
             pltpu.VMEM((2, tall, K // 2), F32),
             pltpu.VMEM((C // 2, 2, tall, K // 2), F32),
             pltpu.VMEM((2, 2, tall, K // 2), F32),
-            dma,
+            dma((6,)), dma,
             dma((R,)), dma((R,)), dma((R,)), dma((R,)),
             dma((C // 2,)), dma((C // 2,)), dma((C // 2,)), dma((C // 2,)),
             dma((C,)), dma((C,)), dma((C,)), dma((C,)),
@@ -313,10 +350,20 @@
             dma, dma,
         ],
         compiler_params=pltpu.CompilerParams(
-            collective_id=0, has_side_effects=True, vmem_limit_bytes=48 * 1024 * 1024
+            collective_id=0, has_side_effects=True, vmem_limit_bytes=60 * 1024 * 1024
         ),
-    )(emb_values, emb_scales, coarse_ids, centroids, codes_one, codes_two, codebook_init)
-    return gap.reshape(N), book_one, book_two, distortion
+    )(
+        emb_values, emb_scales.T, coarse_ids, centroids, codes_one, codes_two,
+        jnp.swapaxes(codebook_init, 1, 2),
+    )
+    gap, book_one, book_two, distortion = pl.pallas_call(
+        write_out,
+        out_shape=tuple(jax.ShapeDtypeStruct(a.shape, a.dtype) for a in results),
+        in_specs=[pl.BlockSpec(memory_space=pl.ANY)] * 4,
+        out_specs=(hbm,) * 4,
+        scratch_shapes=[dma((4,))],
+    )(*results)
+    return gap.reshape(N), jnp.swapaxes(book_one, 1, 2), jnp.swapaxes(book_two, 1, 2), distortion
 
 
 def solution(mesh):

time: 39.1 us -> 39.2 us (level)
  Pallas kernels: 28.4 us -> 38.4 us
  local copies, waits for them, and re-layouts: 9.69 us -> 0 us
    unnamed x16 -> x0, local copies, waits for them, and re-layouts: 9.69 us -> none
    pallas_call x0 -> x1, Pallas kernels: none -> 9.34 us  [on_device(): pl.pallas_call(write_out, out_shape=tuple((jax.ShapeDtypeStruct(a.shape,...]
    pallas_call x1, Pallas kernels: 28.4 us -> 29.1 us  [on_device(): pl.pallas_call(functools.partial(kernel, C, R), out_shape=(jax.ShapeDtype...]
where the time goes in v2:
time: 39.2 us; the launch traced here: 39.1 us
  Pallas kernels  38.4 us (98%)
  between operations  0.64 us (2%)
    pallas_call x1, Pallas kernels, on_device(): pl.pallas_call(functools.partial(kernel, C, R), out_shape=(jax.ShapeDtype...  29.1 us
    pallas_call x1, Pallas kernels, on_device(): pl.pallas_call(write_out, out_shape=tuple((jax.ShapeDtypeStruct(a.shape,...  9.34 us

profile of v2, /device:TPU:0, one launch (start us, length us, event | category | flops | bytes accessed | tf_op | source)
XLA Modules:
  0.0 39.1 jit_solution(3225940482230969619)
XLA Ops:
  0.6 29.1 %shard_map.102 = (f32[1,128]{1,0:T(1,128)}, f32[2,64,256]{2,1,0:T(8,128)}, f32[2,64,256]{2,1,0:T(8,128)}, f32[2,1024]{1,0:T(2,128)}) custom-call(bf16[128,1024]{1,0:T(8,128)(2,1)} %val_hbm.1, bf16[8,128]{1,0:T(8,128)(2,1)} %bitcast.6, s32[4,128]{1,0:T(4,128)} %ids_hbm.1, bf16[2048,1024]{1,0:T(8,128)(2,1)} %cent_hbm.1, s32[2,1024]{1,0:T(2,128)} %one_hbm.1, ...), custom_call_target="tpu_custom_call" | custom-call | tf_op jit(solution)/shard_map/pallas_call | solution.py:308
  29.7 9.3 %shard_map.103 = (f32[1,128]{1,0:T(1,128)}, f32[2,64,256]{2,1,0:T(8,128)}, f32[2,64,256]{2,1,0:T(8,128)}, f32[2,1024]{1,0:T(2,128)}) custom-call(f32[1,128]{1,0:T(1,128)} %get-tuple-element.12.a0, f32[2,64,256]{2,1,0:T(8,128)} %get-tuple-element.13.a1, f32[2,64,256]{2,1,0:T(8,128)} %get-tuple-element.14.a2, f32[2,1024]{1,0:T(2,128)} %get-tuple-element.15.a3), custom_call_target="tpu_custom_call" | custom-call | tf_op jit(solution)/shard_map/pallas_call | solution.py:359

commit v3 on v2

--- a/solution.py
+++ b/solution.py
@@ -282,14 +282,9 @@
         copy.wait_send()
 
 
-def write_out(a0, a1, a2, a3, b0, b1, b2, b3, sems):
-    copies = [
-        pltpu.make_async_copy(a, b, sems.at[i]) for i, (a, b) in enumerate(((a0, b0), (a1, b1), (a2, b2), (a3, b3)))
-    ]
-    for copy in copies:
-        copy.start()
-    for copy in copies:
-        copy.wait()
+def write_out(*refs):
+    for src, dst in zip(refs[:4], refs[4:]):
+        dst[...] = src[...]
 
 
 def on_device(C, R, emb_values, emb_scales, coarse_ids, centroids, codes_one, codes_two, codebook_init):
@@ -359,9 +354,9 @@
     gap, book_one, book_two, distortion = pl.pallas_call(
         write_out,
         out_shape=tuple(jax.ShapeDtypeStruct(a.shape, a.dtype) for a in results),
-        in_specs=[pl.BlockSpec(memory_space=pl.ANY)] * 4,
-        out_specs=(hbm,) * 4,
-        scratch_shapes=[dma((4,))],
+        in_specs=[vmem] * 4,
+        out_specs=(vmem,) * 4,
+        compiler_params=pltpu.CompilerParams(vmem_limit_bytes=60 * 1024 * 1024),
     )(*results)
     return gap.reshape(N), jnp.swapaxes(book_one, 1, 2), jnp.swapaxes(book_two, 1, 2), distortion
 

time: 39.2 us -> 31.6 us (0.81)
  Pallas kernels: 38.4 us -> 30.8 us
    pallas_call x1, Pallas kernels: 9.34 us -> 1.69 us  [on_device(): pl.pallas_call(write_out, out_shape=tuple((jax.ShapeDtypeStruct(a.shape,...]
where the time goes in v3:
time: 31.6 us; the launch traced here: 31.4 us
  Pallas kernels  30.8 us (97%)
  between operations  0.64 us (2%)
    pallas_call x1, Pallas kernels, on_device(): pl.pallas_call(functools.partial(kernel, C, R), out_shape=(jax.ShapeDtype...  29.1 us
    pallas_call x1, Pallas kernels, on_device(): pl.pallas_call(write_out, out_shape=tuple((jax.ShapeDtypeStruct(a.shape,...  1.69 us

profile of v3, /device:TPU:0, one launch (start us, length us, event | category | flops | bytes accessed | tf_op | source)
XLA Modules:
  0.0 31.4 jit_solution(2065816639528775509)
XLA Ops:
  0.6 29.1 %shard_map.102 = (f32[1,128]{1,0:T(1,128)}, f32[2,64,256]{2,1,0:T(8,128)}, f32[2,64,256]{2,1,0:T(8,128)}, f32[2,1024]{1,0:T(2,128)}) custom-call(bf16[128,1024]{1,0:T(8,128)(2,1)} %val_hbm.1, bf16[8,128]{1,0:T(8,128)(2,1)} %bitcast.6, s32[4,128]{1,0:T(4,128)} %ids_hbm.1, bf16[2048,1024]{1,0:T(8,128)(2,1)} %cent_hbm.1, s32[2,1024]{1,0:T(2,128)} %one_hbm.1, ...), custom_call_target="tpu_custom_call" | custom-call | tf_op jit(solution)/shard_map/pallas_call | solution.py:303
  29.7 1.7 %shard_map.103 = (f32[1,128]{1,0:T(1,128)}, f32[2,64,256]{2,1,0:T(8,128)}, f32[2,64,256]{2,1,0:T(8,128)}, f32[2,1024]{1,0:T(2,128)}) custom-call(f32[1,128]{1,0:T(1,128)} %get-tuple-element.12.refs_0_, f32[2,64,256]{2,1,0:T(8,128)} %get-tuple-element.13.refs_1_, f32[2,64,256]{2,1,0:T(8,128)} %get-tuple-element.14.refs_2_, f32[2,1024]{1,0:T(2,128)} %get-tuple-element.15.refs_3_), custom_call_target="tpu_custom_call" | custom-call | tf_op jit(solution)/shard_map/pallas_call | solution.py:354
